TPU v7x, 512 devices: a whole 4x4x16 slice. The times are simulated.
512 devices in a mesh: space: 32 (over y_hi, z), rep: 16 (over y_lo, x, core).
Axes of the slice: x: 4, y: 4 (y_hi: 2, y_lo: 2; y = y_hi * 2 + y_lo), z: 16, core: 2. Of those that a mesh axis runs over, the one named last changes fastest.
Arguments:
- volumes: bfloat16 [16, 32, 8, 4, 16, 256], P('rep', 'space'), may hold values from -6 to 6
- grad_parts: bfloat16 [16, 2, 6912, 256], P('rep', None, 'space'), may hold values from -6 to 6
- master_weights: float32 [2, 6912, 256], P(None, 'space'), may hold values from -0.078125 to 0.078125
- moment_first: float32 [16, 2, 6912, 256], P('rep', None, 'space'), may hold values from -12 to 12
- moment_second: float32 [16, 2, 6912, 256], P('rep', None, 'space'), may hold values from 1 to 30
- owner: int32 [2, 32], replicated, may hold values from 0 to 15
Outputs:
- features: bfloat16 [16, 32, 8, 4, 16, 256], P('rep', 'space')
- new_weights: float32 [2, 1769472], P(None, ('space', 'rep'))
- moment_first_out: float32 [16, 2, 6912, 256], P('rep', None, 'space')
- moment_second_out: float32 [16, 2, 6912, 256], P('rep', None, 'space')
Inputs may be any that keep to these rules, and one draw needn't show every extreme that they name: owner[f, p] is the replica whose state slot holds the optimizer state of panel p of filter f, rows p * 216 to (p + 1) * 216 - 1; replicas may own unequal numbers of panels.
All inputs are finite; a program needn't handle non-finite values.
Results may differ from a plain program's by a relative error of at most 0.0095.
Values may be sent and summed in bfloat16 or wider, within the bound.
A program may use at most 64 MiB of HBM per device.

v0:
```python
import jax
import jax.numpy as jnp
from jax import lax
from jax.sharding import PartitionSpec as P

GY = 2
GZ = 2
PANEL_ROWS = 216


def passed_along(value, axis, steps):
    count = lax.axis_size(axis)
    first, last = (max(0, -steps), min(count, count - steps))
    return lax.ppermute(value, axis, [(source, source + steps) for source in range(first, last)])


def over_pieces(array, axis):
    blocks = lax.all_gather(array, axis).astype(jnp.float32)
    return blocks.sum(axis=0)


def from_root(array, axis, root):
    return lax.dynamic_index_in_dim(lax.all_gather(array, axis), root, 0, keepdims=False)


def neighbour(slab, offset):
    return passed_along(slab, "space", offset)


def keep_when(flag, slab):
    return jnp.where(flag, slab, jnp.zeros_like(slab))


def side_slab(array, dim, side):
    length = array.shape[dim]
    if side < 0:
        return lax.slice_in_dim(array, length - 1, length, 1, dim)
    return lax.slice_in_dim(array, 0, 1, 1, dim)


def extend_brick(brick, coords, strides, grid):
    lows = [coords[d] > 0 for d in range(3)]
    highs = [coords[d] < grid[d] - 1 for d in range(3)]
    current = brick
    for dim in range(3):
        lower = keep_when(lows[dim], neighbour(side_slab(current, dim, -1), strides[dim]))
        upper = keep_when(highs[dim], neighbour(side_slab(current, dim, 1), -strides[dim]))
        current = jnp.concatenate([lower, current, upper], axis=dim)
    return current


def convolve(extended, filter_rows):
    extent_x = extended.shape[0] - 2
    extent_y = extended.shape[1] - 2
    extent_z = extended.shape[2] - 2
    channels = extended.shape[3]
    summed = jnp.zeros((extent_x * extent_y * extent_z, filter_rows.shape[1]), jnp.float32)
    for shift_x in range(3):
        for shift_y in range(3):
            for shift_z in range(3):
                tap_index = (shift_x * 3 + shift_y) * 3 + shift_z
                window = extended[
                    shift_x : shift_x + extent_x,
                    shift_y : shift_y + extent_y,
                    shift_z : shift_z + extent_z,
                ]
                weights_tap = filter_rows[tap_index * channels : (tap_index + 1) * channels]
                summed = summed + jnp.dot(
                    window.reshape(-1, channels), weights_tap, preferred_element_type=jnp.float32
                )
    return summed.reshape(extent_x, extent_y, extent_z, -1)


def shards(volumes, grad_parts, master_weights, moment_first, moment_second, owner):
    filter_count = master_weights.shape[0]
    rows_dev = master_weights.shape[1]
    channels = master_weights.shape[2]
    panels_dev = rows_dev // PANEL_ROWS
    space_pos = lax.axis_index("space")
    rep_pos = lax.axis_index("rep")
    summed_grad = over_pieces(grad_parts[0].astype(jnp.float32).astype(jnp.bfloat16), "rep").astype(
        jnp.float32
    )
    first_new = 0.9 * moment_first[0] + 0.1 * summed_grad
    second_new = 0.95 * moment_second[0] + 0.05 * (summed_grad * summed_grad)
    owner_local = lax.dynamic_slice_in_dim(owner, space_pos * panels_dev, panels_dev, 1)
    owner_rows = jnp.repeat(owner_local, PANEL_ROWS, axis=1)
    owned = (owner_rows == rep_pos)[:, :, None]
    first_out = jnp.where(owned, first_new, moment_first[0])[None]
    second_out = jnp.where(owned, second_new, moment_second[0])[None]
    corr_one = 1.0 - 0.9**10
    corr_two = 1.0 - 0.95**10
    update = first_new / corr_one / (jnp.sqrt(second_new / corr_two) + 1e-08) + 0.1 * master_weights
    candidate = master_weights - 0.004 * update
    per_filter = []
    for filter_index in range(filter_count):
        slab = candidate[filter_index, 0:PANEL_ROWS]
        slabs = from_root(slab.astype(jnp.bfloat16), "rep", owner_local[filter_index, 0]).astype(
            slab.dtype
        )
        per_filter.append(slabs)
    new_master = jnp.stack(per_filter)
    share_len = rows_dev * channels // lax.axis_size("rep")
    new_weights = lax.dynamic_slice_in_dim(
        new_master.reshape(filter_count, -1), rep_pos * share_len, share_len, 1
    )
    filters = lax.all_gather(new_master.astype(jnp.bfloat16), "space", axis=1, tiled=True)
    grid = (lax.axis_size("space") // (GY * GZ), GY, GZ)
    strides = (GY * GZ, GZ, 1)
    coords = (space_pos // (GY * GZ), space_pos // GZ % GY, space_pos % GZ)
    brick = volumes[0, 0]
    hidden = jax.nn.gelu(
        convolve(extend_brick(brick, coords, strides, grid), filters[0]), approximate=True
    ).astype(jnp.bfloat16)
    output = jax.nn.gelu(
        convolve(extend_brick(hidden, coords, strides, grid), filters[1]), approximate=True
    ).astype(jnp.bfloat16)
    return (output[None, None], new_weights, first_out, second_out)


def solution(mesh):
    placed = (
        P("rep", "space", None, None, None, None),
        P("rep", None, "space", None),
        P(None, "space", None),
        P("rep", None, "space", None),
        P("rep", None, "space", None),
        P(),
    )
    return jax.shard_map(
        shards,
        mesh=mesh,
        in_specs=placed,
        out_specs=(
            P("rep", "space", None, None, None, None),
            P(None, ("space", "rep")),
            P("rep", None, "space", None),
            P("rep", None, "space", None),
        ),
        check_vma=False,
    )
```

profile of v0, /device:TPU:24, one launch (start us, length us, event | category | flops | bytes accessed | tf_op | source)
XLA Modules:
  0.0 415.0 jit_solution(16245634699472826510)
XLA Ops:
  8.0 50.1 %all-gather.5.cloned.1.call-done = bf16[16,2,216,256]{3,2,1,0:T(8,128)(2,1)} async-done(((bf16[1,2,216,256]{3,2,1,0:T(8,128)(2,1)}), bf16[16,2,216,256]{3,2,1,0:T(8,128)(2,1)}) %all-gather.5.cloned.1.call-update) | async-done | bytes 3538960 | tf_op jit(solution)/shard_map/all_gather | solution.py:18
  58.1 2.6 convert_reduce_fusion
  60.7 1.6 fusion.43
  63.8 0.9 compare_reduce_fusion
  69.1 35.6 %all-gather.9.cloned.1.call-done = bf16[16,216,256]{2,1,0:T(8,128)(2,1)} async-done(((bf16[1,216,256]{2,1,0:T(8,128)(2,1)}), bf16[16,216,256]{2,1,0:T(8,128)(2,1)}) %all-gather.9.cloned.1.call-update) | async-done | bytes 1769488 | tf_op jit(solution)/shard_map/all_gather | solution.py:23
  104.7 0.9 constant_dynamic-slice_fusion
  105.6 43.1 %all-gather.7.cloned.1.call-done = bf16[16,216,256]{2,1,0:T(8,128)(2,1)} async-done(((bf16[1,216,256]{2,1,0:T(8,128)(2,1)}), bf16[16,216,256]{2,1,0:T(8,128)(2,1)}) %all-gather.7.cloned.1.call-update) | async-done | bytes 1769488 | tf_op jit(solution)/shard_map/all_gather | solution.py:23
  148.7 0.9 constant_dynamic-slice_fusion.1
  149.6 0.7 pad_maximum_fusion.8
  150.3 7.6 %collective-permute-start = (bf16[1,4,16,256]{3,2,1,0:T(8,128)(2,1)S(1)}, bf16[1,4,16,256]{3,2,1,0:T(8,128)(2,1)S(1)}, u32[]{:S(2)}, u32[]{:S(2)}) collective-permute-start(bf16[1,4,16,256]{3,2,1,0:T(8,128)(2,1)S(1)} %get-tuple-element.78), channel_id=1, source_target_pairs={{0,64},{16,80},{32,96},{48,112},{64,128},{80,144},{96,160},{112,17... | collective-permute-start | bytes 98312 | tf_op jit(solution)/shard_map/ppermute | solution.py:14
  158.0 4.5 %collective-permute-start.1 = (bf16[1,4,16,256]{3,2,1,0:T(8,128)(2,1)S(1)}, bf16[1,4,16,256]{3,2,1,0:T(8,128)(2,1)S(1)}, u32[]{:S(2)}, u32[]{:S(2)}) collective-permute-start(bf16[1,4,16,256]{3,2,1,0:T(8,128)(2,1)S(1)} %get-tuple-element.79), channel_id=1, source_target_pairs={{64,0},{80,16},{96,32},{112,48},{128,64},{144,80},{160,96},{176,11... | collective-permute-start | bytes 98312 | tf_op jit(solution)/shard_map/ppermute | solution.py:14
  162.6 5.5 %collective-permute-done.1 = bf16[1,4,16,256]{3,2,1,0:T(8,128)(2,1)S(1)} collective-permute-done((bf16[1,4,16,256]{3,2,1,0:T(8,128)(2,1)S(1)}, bf16[1,4,16,256]{3,2,1,0:T(8,128)(2,1)S(1)}, u32[]{:S(2)}, u32[]{:S(2)}) %collective-permute-start.1) | collective-permute-done | bytes 32800 | tf_op jit(solution)/shard_map/ppermute | solution.py:14
  168.1 4.4 %collective-permute-start.2 = (bf16[10,1,16,256]{3,2,1,0:T(8,128)(2,1)S(1)}, bf16[10,1,16,256]{3,2,1,0:T(8,128)(2,1)S(1)}, u32[]{:S(2)}, u32[]{:S(2)}) collective-permute-start(bf16[10,1,16,256]{3,2,1,0:T(8,128)(2,1)S(1)} %get-tuple-element.70), channel_id=1, source_target_pairs={{0,32},{16,48},{32,64},{48,80},{64,96},{80,112},{96,128},{112,144}... | collective-permute-start | bytes 245768 | tf_op jit(solution)/shard_map/ppermute | solution.py:14
  172.5 6.0 %collective-permute-start.3 = (bf16[10,1,16,256]{3,2,1,0:T(8,128)(2,1)S(1)}, bf16[10,1,16,256]{3,2,1,0:T(8,128)(2,1)S(1)}, u32[]{:S(2)}, u32[]{:S(2)}) collective-permute-start(bf16[10,1,16,256]{3,2,1,0:T(8,128)(2,1)S(1)} %get-tuple-element.71), channel_id=1, source_target_pairs={{32,0},{48,16},{64,32},{80,48},{96,64},{112,80},{128,96},{144,112}... | collective-permute-start | bytes 245768 | tf_op jit(solution)/shard_map/ppermute | solution.py:14
  178.5 0.8 pad_maximum_fusion.6
  179.5 4.6 %collective-permute-done.3 = bf16[10,1,16,256]{3,2,1,0:T(8,128)(2,1)S(1)} collective-permute-done((bf16[10,1,16,256]{3,2,1,0:T(8,128)(2,1)S(1)}, bf16[10,1,16,256]{3,2,1,0:T(8,128)(2,1)S(1)}, u32[]{:S(2)}, u32[]{:S(2)}) %collective-permute-start.3) | collective-permute-done | bytes 81952 | tf_op jit(solution)/shard_map/ppermute | solution.py:14
  184.2 6.7 %collective-permute-start.5 = (bf16[10,6,1,256]{3,2,1,0:T(2,128)(2,1)S(1)}, bf16[10,6,1,256]{3,2,1,0:T(2,128)(2,1)S(1)}, u32[]{:S(2)}, u32[]{:S(2)}) collective-permute-start(bf16[10,6,1,256]{3,2,1,0:T(2,128)(2,1)S(1)} %get-tuple-element.48), channel_id=1, source_target_pairs={{16,0},{32,16},{48,32},{64,48},{80,64},{96,80},{112,96},{128,112},... | collective-permute-start | bytes 92168 | tf_op jit(solution)/shard_map/ppermute | solution.py:14
  190.8 1.9 collective-permute-start.4
  192.9 1.0 fusion.71
  194.0 7.2 %collective-permute-done.4 = bf16[10,6,1,256]{3,2,1,0:T(2,128)(2,1)S(1)} collective-permute-done((bf16[10,6,1,256]{3,2,1,0:T(2,128)(2,1)S(1)}, bf16[10,6,1,256]{3,2,1,0:T(2,128)(2,1)S(1)}, u32[]{:S(2)}, u32[]{:S(2)}) %collective-permute-start.4) | collective-permute-done | bytes 30752 | tf_op jit(solution)/shard_map/ppermute | solution.py:14
  201.7 1.9 fusion.67
  203.6 1.1 fusion.33
  204.7 0.9 fusion.130
  205.8 0.9 fusion.129
  206.7 0.9 copy.13
  207.6 127.3 %all-gather.11.cloned.1.call-done = bf16[2,6912,256]{2,1,0:T(8,128)(2,1)} async-done(((bf16[2,216,256]{2,1,0:T(8,128)(2,1)}), bf16[2,6912,256]{2,1,0:T(8,128)(2,1)}) %all-gather.11.cloned.1.call-update) | async-done | bytes 7077904 | tf_op jit(solution)/shard_map/all_gather | solution.py:107
  334.9 1.3 fusion.55
  336.2 1.7 fusion.52
  337.9 1.1 fusion.51
  339.0 1.2 fusion.54
  340.2 1.1 fusion.57
  341.3 1.2 fusion.58
  342.5 1.2 fusion.56
  343.7 1.1 fusion.53
  345.1 1.2 convolution_add_fusion.42
  346.6 1.2 convolution_add_fusion.40
  347.8 1.2 convolution_add_fusion.39
  352.7 4.8 %collective-permute-start.6 = (bf16[1,4,16,256]{3,2,1,0:T(8,128)(2,1)S(1)}, bf16[1,4,16,256]{3,2,1,0:T(8,128)(2,1)S(1)}, u32[]{:S(2)}, u32[]{:S(2)}) collective-permute-start(bf16[1,4,16,256]{3,2,1,0:T(8,128)(2,1)S(1)} %get-tuple-element.74), channel_id=1, source_target_pairs={{0,64},{16,80},{32,96},{48,112},{64,128},{80,144},{96,160},{112,17... | collective-permute-start | bytes 98312 | tf_op jit(solution)/shard_map/ppermute | solution.py:14
  357.6 0.7 fusion.60
  358.3 7.3 %collective-permute-start.7 = (bf16[1,4,16,256]{3,2,1,0:T(8,128)(2,1)S(1)}, bf16[1,4,16,256]{3,2,1,0:T(8,128)(2,1)S(1)}, u32[]{:S(2)}, u32[]{:S(2)}) collective-permute-start(bf16[1,4,16,256]{3,2,1,0:T(8,128)(2,1)S(1)} %get-tuple-element.75), channel_id=1, source_target_pairs={{64,0},{80,16},{96,32},{112,48},{128,64},{144,80},{160,96},{176,11... | collective-permute-start | bytes 98312 | tf_op jit(solution)/shard_map/ppermute | solution.py:14
  365.6 2.4 collective-permute-done.7
  368.0 4.0 collective-permute-start.8
  372.0 8.4 %collective-permute-start.9 = (bf16[10,1,16,256]{3,2,1,0:T(8,128)(2,1)S(1)}, bf16[10,1,16,256]{3,2,1,0:T(8,128)(2,1)S(1)}, u32[]{:S(2)}, u32[]{:S(2)}) collective-permute-start(bf16[10,1,16,256]{3,2,1,0:T(8,128)(2,1)S(1)} %get-tuple-element.67), channel_id=1, source_target_pairs={{32,0},{48,16},{64,32},{80,48},{96,64},{112,80},{128,96},{144,112}... | collective-permute-start | bytes 245768 | tf_op jit(solution)/shard_map/ppermute | solution.py:14
  380.9 1.9 collective-permute-done.9
  383.1 7.1 %collective-permute-start.11 = (bf16[10,6,1,256]{3,2,1,0:T(2,128)(2,1)S(1)}, bf16[10,6,1,256]{3,2,1,0:T(2,128)(2,1)S(1)}, u32[]{:S(2)}, u32[]{:S(2)}) collective-permute-start(bf16[10,6,1,256]{3,2,1,0:T(2,128)(2,1)S(1)} %get-tuple-element.44), channel_id=1, source_target_pairs={{16,0},{32,16},{48,32},{64,48},{80,64},{96,80},{112,96},{128,112},... | collective-permute-start | bytes 92168 | tf_op jit(solution)/shard_map/ppermute | solution.py:14
  390.2 2.1 collective-permute-start.10
  392.6 7.4 %collective-permute-done.10 = bf16[10,6,1,256]{3,2,1,0:T(2,128)(2,1)S(1)} collective-permute-done((bf16[10,6,1,256]{3,2,1,0:T(2,128)(2,1)S(1)}, bf16[10,6,1,256]{3,2,1,0:T(2,128)(2,1)S(1)}, u32[]{:S(2)}, u32[]{:S(2)}) %collective-permute-start.10) | collective-permute-done | bytes 30752 | tf_op jit(solution)/shard_map/ppermute | solution.py:14
  407.6 0.9 fusion.32
  (124 shorter events, 16.4 us)
Async XLA Ops:
  7.2 143.1 %copy-start = (bf16[1,1,8,4,16,256]{5,4,3,2,1,0:T(8,128)(2,1)S(1)}, bf16[1,1,8,4,16,256]{5,4,3,2,1,0:T(8,128)(2,1)}, u32[]{:S(2)}) copy-start(bf16[1,1,8,4,16,256]{5,4,3,2,1,0:T(8,128)(2,1)} %param.6) | copy-start | bytes 786436
  7.2 50.9 %all-gather.5.cloned.1.call-start = ((), (), s32[]{:S(2)}) async-start(), calls=%async_computation | async-start | bytes 3760128 | tf_op jit(solution)/shard_map/all_gather | solution.py:18
  7.9 96.7 %all-gather.9.cloned.1.call-start = ((), (), s32[]{:S(2)}) async-start(), calls=%async_computation.2 | async-start | bytes 1880064 | tf_op jit(solution)/shard_map/all_gather | solution.py:23
  63.0 85.6 %all-gather.7.cloned.1.call-start = ((), (), s32[]{:S(2)}) async-start(), calls=%async_computation.1 | async-start | bytes 1880064 | tf_op jit(solution)/shard_map/all_gather | solution.py:23
  63.8 271.1 %all-gather.11.cloned.1.call-start = ((), (), s32[]{:S(2)}) async-start(), calls=%async_computation.3 | async-start | bytes 7299072 | tf_op jit(solution)/shard_map/all_gather | solution.py:107
  150.3 12.3 %collective-permute-start = (bf16[1,4,16,256]{3,2,1,0:T(8,128)(2,1)S(1)}, bf16[1,4,16,256]{3,2,1,0:T(8,128)(2,1)S(1)}, u32[]{:S(2)}, u32[]{:S(2)}) collective-permute-start(bf16[1,4,16,256]{3,2,1,0:T(8,128)(2,1)S(1)} %get-tuple-element.78), channel_id=1, source_target_pairs={{0,64},{16,80},{32,96},{48,112},{64,128},{80,144},{96,160},{112,17... | collective-permute-start | bytes 98312 | tf_op jit(solution)/shard_map/ppermute | solution.py:14
  158.0 10.1 %collective-permute-start.1 = (bf16[1,4,16,256]{3,2,1,0:T(8,128)(2,1)S(1)}, bf16[1,4,16,256]{3,2,1,0:T(8,128)(2,1)S(1)}, u32[]{:S(2)}, u32[]{:S(2)}) collective-permute-start(bf16[1,4,16,256]{3,2,1,0:T(8,128)(2,1)S(1)} %get-tuple-element.79), channel_id=1, source_target_pairs={{64,0},{80,16},{96,32},{112,48},{128,64},{144,80},{160,96},{176,11... | collective-permute-start | bytes 98312 | tf_op jit(solution)/shard_map/ppermute | solution.py:14
  168.1 11.3 %collective-permute-start.2 = (bf16[10,1,16,256]{3,2,1,0:T(8,128)(2,1)S(1)}, bf16[10,1,16,256]{3,2,1,0:T(8,128)(2,1)S(1)}, u32[]{:S(2)}, u32[]{:S(2)}) collective-permute-start(bf16[10,1,16,256]{3,2,1,0:T(8,128)(2,1)S(1)} %get-tuple-element.70), channel_id=1, source_target_pairs={{0,32},{16,48},{32,64},{48,80},{64,96},{80,112},{96,128},{112,144}... | collective-permute-start | bytes 245768 | tf_op jit(solution)/shard_map/ppermute | solution.py:14
  172.5 11.6 %collective-permute-start.3 = (bf16[10,1,16,256]{3,2,1,0:T(8,128)(2,1)S(1)}, bf16[10,1,16,256]{3,2,1,0:T(8,128)(2,1)S(1)}, u32[]{:S(2)}, u32[]{:S(2)}) collective-permute-start(bf16[10,1,16,256]{3,2,1,0:T(8,128)(2,1)S(1)} %get-tuple-element.71), channel_id=1, source_target_pairs={{32,0},{48,16},{64,32},{80,48},{96,64},{112,80},{128,96},{144,112}... | collective-permute-start | bytes 245768 | tf_op jit(solution)/shard_map/ppermute | solution.py:14
  184.2 9.7 %collective-permute-start.5 = (bf16[10,6,1,256]{3,2,1,0:T(2,128)(2,1)S(1)}, bf16[10,6,1,256]{3,2,1,0:T(2,128)(2,1)S(1)}, u32[]{:S(2)}, u32[]{:S(2)}) collective-permute-start(bf16[10,6,1,256]{3,2,1,0:T(2,128)(2,1)S(1)} %get-tuple-element.48), channel_id=1, source_target_pairs={{16,0},{32,16},{48,32},{64,48},{80,64},{96,80},{112,96},{128,112},... | collective-permute-start | bytes 92168 | tf_op jit(solution)/shard_map/ppermute | solution.py:14
  190.8 10.3 %collective-permute-start.4 = (bf16[10,6,1,256]{3,2,1,0:T(2,128)(2,1)S(1)}, bf16[10,6,1,256]{3,2,1,0:T(2,128)(2,1)S(1)}, u32[]{:S(2)}, u32[]{:S(2)}) collective-permute-start(bf16[10,6,1,256]{3,2,1,0:T(2,128)(2,1)S(1)} %get-tuple-element.49), channel_id=1, source_target_pairs={{0,16},{16,32},{32,48},{48,64},{64,80},{80,96},{96,112},{112,128},... | collective-permute-start | bytes 92168 | tf_op jit(solution)/shard_map/ppermute | solution.py:14
  192.9 10.7 %copy-start.2 = (f32[1,2,216,256]{3,2,1,0:T(8,128)S(1)}, f32[1,2,216,256]{3,2,1,0:T(8,128)}, u32[]{:S(2)}) copy-start(f32[1,2,216,256]{3,2,1,0:T(8,128)} %param.10) | copy-start | bytes 1327108
  192.9 10.7 %copy-start.3 = (f32[1,2,216,256]{3,2,1,0:T(8,128)S(1)}, f32[1,2,216,256]{3,2,1,0:T(8,128)}, u32[]{:S(2)}) copy-start(f32[1,2,216,256]{3,2,1,0:T(8,128)} %param.9) | copy-start | bytes 1327108
  207.6 141.4 %copy-start.14 = (bf16[8,4,16,256]{3,2,1,0:T(8,128)(2,1)S(1)}, bf16[8,4,16,256]{3,2,1,0:T(8,128)(2,1)}, u32[]{:S(2)}) copy-start(bf16[8,4,16,256]{3,2,1,0:T(8,128)(2,1)} %get-tuple-element.31) | copy-start | bytes 786436
  334.9 10.0 %copy-start.1 = (bf16[2,6912,256]{2,1,0:T(8,128)(2,1)S(1)}, bf16[2,6912,256]{2,1,0:T(8,128)(2,1)}, u32[]{:S(2)}) copy-start(bf16[2,6912,256]{2,1,0:T(8,128)(2,1)} %all-gather.11.cloned.1.call-done) | copy-start | bytes 21233668
  334.9 11.4 %copy-start.15 = (bf16[8,4,16,256]{3,2,1,0:T(8,128)(2,1)S(1)}, bf16[8,4,16,256]{3,2,1,0:T(8,128)(2,1)}, u32[]{:S(2)}) copy-start(bf16[8,4,16,256]{3,2,1,0:T(8,128)(2,1)} %get-tuple-element.32) | copy-start | bytes 786436
  336.2 13.0 %copy-start.13 = (bf16[8,4,16,256]{3,2,1,0:T(8,128)(2,1)S(1)}, bf16[8,4,16,256]{3,2,1,0:T(8,128)(2,1)}, u32[]{:S(2)}) copy-start(bf16[8,4,16,256]{3,2,1,0:T(8,128)(2,1)} %get-tuple-element.86) | copy-start | bytes 786436
  339.0 10.4 %copy-start.5 = (bf16[8,4,16,256]{3,2,1,0:T(8,128)(2,1)S(1)}, bf16[8,4,16,256]{3,2,1,0:T(8,128)(2,1)}, u32[]{:S(2)}) copy-start(bf16[8,4,16,256]{3,2,1,0:T(8,128)(2,1)} %get-tuple-element.60) | copy-start | bytes 786436
  341.3 8.4 %copy-start.12 = (bf16[8,4,16,256]{3,2,1,0:T(8,128)(2,1)S(1)}, bf16[8,4,16,256]{3,2,1,0:T(8,128)(2,1)}, u32[]{:S(2)}) copy-start(bf16[8,4,16,256]{3,2,1,0:T(8,128)(2,1)} %get-tuple-element.30) | copy-start | bytes 786436
  342.5 7.4 %copy-start.11 = (bf16[8,4,16,256]{3,2,1,0:T(8,128)(2,1)S(1)}, bf16[8,4,16,256]{3,2,1,0:T(8,128)(2,1)}, u32[]{:S(2)}) copy-start(bf16[8,4,16,256]{3,2,1,0:T(8,128)(2,1)} %get-tuple-element.87) | copy-start | bytes 786436
  344.8 5.4 %copy-start.4 = (bf16[8,4,16,256]{3,2,1,0:T(8,128)(2,1)S(1)}, bf16[8,4,16,256]{3,2,1,0:T(8,128)(2,1)}, u32[]{:S(2)}) copy-start(bf16[8,4,16,256]{3,2,1,0:T(8,128)(2,1)} %get-tuple-element.95) | copy-start | bytes 786436
  345.1 5.3 %copy-start.10 = (bf16[8,4,16,256]{3,2,1,0:T(8,128)(2,1)S(1)}, bf16[8,4,16,256]{3,2,1,0:T(8,128)(2,1)}, u32[]{:S(2)}) copy-start(bf16[8,4,16,256]{3,2,1,0:T(8,128)(2,1)} %get-tuple-element.29) | copy-start | bytes 786436
  346.3 4.4 %copy-start.9 = (bf16[8,4,16,256]{3,2,1,0:T(8,128)(2,1)S(1)}, bf16[8,4,16,256]{3,2,1,0:T(8,128)(2,1)}, u32[]{:S(2)}) copy-start(bf16[8,4,16,256]{3,2,1,0:T(8,128)(2,1)} %get-tuple-element.88) | copy-start | bytes 786436
  349.4 1.9 copy-start.16
  349.7 1.9 copy-start.8
  349.9 1.9 copy-start.7
  350.4 1.8 copy-start.6
  350.9 6.6 %copy-start.17 = (bf16[1,1,216,256]{3,1,2,0:T(2,128)(2,1)S(1)}, bf16[1,1,216,256]{3,1,2,0:T(2,128)(2,1)}, u32[]{:S(2)}) copy-start(bf16[1,1,216,256]{3,1,2,0:T(2,128)(2,1)} %copy.13) | copy-start | bytes 331780
  352.7 12.9 %collective-permute-start.6 = (bf16[1,4,16,256]{3,2,1,0:T(8,128)(2,1)S(1)}, bf16[1,4,16,256]{3,2,1,0:T(8,128)(2,1)S(1)}, u32[]{:S(2)}, u32[]{:S(2)}) collective-permute-start(bf16[1,4,16,256]{3,2,1,0:T(8,128)(2,1)S(1)} %get-tuple-element.74), channel_id=1, source_target_pairs={{0,64},{16,80},{32,96},{48,112},{64,128},{80,144},{96,160},{112,17... | collective-permute-start | bytes 98312 | tf_op jit(solution)/shard_map/ppermute | solution.py:14
  358.3 9.7 %collective-permute-start.7 = (bf16[1,4,16,256]{3,2,1,0:T(8,128)(2,1)S(1)}, bf16[1,4,16,256]{3,2,1,0:T(8,128)(2,1)S(1)}, u32[]{:S(2)}, u32[]{:S(2)}) collective-permute-start(bf16[1,4,16,256]{3,2,1,0:T(8,128)(2,1)S(1)} %get-tuple-element.75), channel_id=1, source_target_pairs={{64,0},{80,16},{96,32},{112,48},{128,64},{144,80},{160,96},{176,11... | collective-permute-start | bytes 98312 | tf_op jit(solution)/shard_map/ppermute | solution.py:14
  368.0 12.9 %collective-permute-start.8 = (bf16[10,1,16,256]{3,2,1,0:T(8,128)(2,1)S(1)}, bf16[10,1,16,256]{3,2,1,0:T(8,128)(2,1)S(1)}, u32[]{:S(2)}, u32[]{:S(2)}) collective-permute-start(bf16[10,1,16,256]{3,2,1,0:T(8,128)(2,1)S(1)} %get-tuple-element.66), channel_id=1, source_target_pairs={{0,32},{16,48},{32,64},{48,80},{64,96},{80,112},{96,128},{112,144}... | collective-permute-start | bytes 245768 | tf_op jit(solution)/shard_map/ppermute | solution.py:14
  372.0 10.8 %collective-permute-start.9 = (bf16[10,1,16,256]{3,2,1,0:T(8,128)(2,1)S(1)}, bf16[10,1,16,256]{3,2,1,0:T(8,128)(2,1)S(1)}, u32[]{:S(2)}, u32[]{:S(2)}) collective-permute-start(bf16[10,1,16,256]{3,2,1,0:T(8,128)(2,1)S(1)} %get-tuple-element.67), channel_id=1, source_target_pairs={{32,0},{48,16},{64,32},{80,48},{96,64},{112,80},{128,96},{144,112}... | collective-permute-start | bytes 245768 | tf_op jit(solution)/shard_map/ppermute | solution.py:14
  383.1 9.4 %collective-permute-start.11 = (bf16[10,6,1,256]{3,2,1,0:T(2,128)(2,1)S(1)}, bf16[10,6,1,256]{3,2,1,0:T(2,128)(2,1)S(1)}, u32[]{:S(2)}, u32[]{:S(2)}) collective-permute-start(bf16[10,6,1,256]{3,2,1,0:T(2,128)(2,1)S(1)} %get-tuple-element.44), channel_id=1, source_target_pairs={{16,0},{32,16},{48,32},{64,48},{80,64},{96,80},{112,96},{128,112},... | collective-permute-start | bytes 92168 | tf_op jit(solution)/shard_map/ppermute | solution.py:14
  390.2 9.7 %collective-permute-start.10 = (bf16[10,6,1,256]{3,2,1,0:T(2,128)(2,1)S(1)}, bf16[10,6,1,256]{3,2,1,0:T(2,128)(2,1)S(1)}, u32[]{:S(2)}, u32[]{:S(2)}) collective-permute-start(bf16[10,6,1,256]{3,2,1,0:T(2,128)(2,1)S(1)} %get-tuple-element.45), channel_id=1, source_target_pairs={{0,16},{16,32},{32,48},{48,64},{64,80},{80,96},{96,112},{112,128},... | collective-permute-start | bytes 92168 | tf_op jit(solution)/shard_map/ppermute | solution.py:14
Sparse Core Ops, SparseCore 0:
  10.1 47.9 all-gather.4
  63.2 41.4 all-gather.8
  107.4 41.2 all-gather.6
  151.6 183.2 all-gather.10
where the time goes:
time: 416 us; the launch traced here: 415 us
  waiting for transfers between devices  287 us (69%)
  starting transfers between devices  65 us (16%)
  matrix products  23.4 us (6%)
  between operations  18.6 us (4%)
  other arithmetic  11.2 us (3%)
  local copies, waits for them, and re-layouts  9.75 us (2%)
    all_gather x1, waiting for transfers between devices, shards(): lax.all_gather(new_master.astype(jnp.bfloat16), 'space', axis=1, tiled=True)  127 us
    all_gather x2, waiting for transfers between devices, from_root(): lax.all_gather(array, axis)  78.7 us
    ppermute x12, starting transfers between devices, passed_along(): lax.ppermute(value, axis, [(source, source + steps) for source in range(f...  64.9 us
    all_gather x1, waiting for transfers between devices, over_pieces(): blocks = lax.all_gather(array, axis).astype(jnp.float32)  50.1 us
    ppermute x12, waiting for transfers between devices, passed_along(): lax.ppermute(value, axis, [(source, source + steps) for source in range(f...  29.5 us
    dot_general x54, matrix products, convolve(): jnp.dot(window.reshape(-1, channels), weights_tap, preferred_element_type...  23.4 us
  transfers between devices with their start and end apart: 16, of which 12 were waited for; matrix products, arithmetic and copies ran while one was open for 3% of the time, Pallas kernels for 0%

commit v1 on v0

--- a/solution.py
+++ b/solution.py
@@ -104,7 +104,11 @@
     new_weights = lax.dynamic_slice_in_dim(
         new_master.reshape(filter_count, -1), rep_pos * share_len, share_len, 1
     )
-    filters = lax.all_gather(new_master.astype(jnp.bfloat16), "space", axis=1, tiled=True)
+    a0 = new_master.astype(jnp.bfloat16)
+    step_out = lax.all_to_all(
+        jnp.stack([a0 for _ in range(lax.axis_size("space"))], axis=0), "space", 0, 0
+    )
+    filters = jnp.concatenate(step_out, axis=1)
     grid = (lax.axis_size("space") // (GY * GZ), GY, GZ)
     strides = (GY * GZ, GZ, 1)
     coords = (space_pos // (GY * GZ), space_pos // GZ % GY, space_pos % GZ)

time: 416 us -> 581 us (1.40)
  waiting for transfers between devices: 287 us -> 446 us
  starting transfers between devices: 65 us -> 77.2 us
  matrix products: 23.4 us -> 12.5 us
  local copies, waits for them, and re-layouts: 9.75 us -> 16.5 us
    ppermute x12, waiting for transfers between devices: 29.5 us -> 316 us  [passed_along(): lax.ppermute(value, axis, [(source, source + steps) for source in range(f...]
    all_gather x1 -> x0, waiting for transfers between devices: 127 us -> none  [shards(): lax.all_gather(new_master.astype(jnp.bfloat16), 'space', axis=1, tiled=True)]
    all_to_all x0 -> x1, starting transfers between devices: none -> 15.5 us  [shards(): lax.all_to_all(jnp.stack([a0 for _ in range(lax.axis_size('space'))], axi...]
    dot_general x54, matrix products: 23.4 us -> 12.5 us  [convolve(): jnp.dot(window.reshape(-1, channels), weights_tap, preferred_element_type...]
  transfers between devices with their start and end apart: 16 -> 16, of which waited for: 12 -> 10; matrix products, arithmetic and copies ran while one was open for 3% -> 2% of each run, Pallas kernels for 0% -> 0%
where the time goes in v1:
time: 581 us; the launch traced here: 580 us
  waiting for transfers between devices  446 us (77%)
  starting transfers between devices  77.2 us (13%)
  between operations  18.7 us (3%)
  local copies, waits for them, and re-layouts  16.5 us (3%)
  matrix products  12.5 us (2%)
  other arithmetic  8.51 us (1%)
    ppermute x12, waiting for transfers between devices, passed_along(): lax.ppermute(value, axis, [(source, source + steps) for source in range(f...  316 us
    all_gather x2, waiting for transfers between devices, from_root(): lax.all_gather(array, axis)  79.4 us
    ppermute x12, starting transfers between devices, passed_along(): lax.ppermute(value, axis, [(source, source + steps) for source in range(f...  61.6 us
    all_gather x1, waiting for transfers between devices, over_pieces(): blocks = lax.all_gather(array, axis).astype(jnp.float32)  50.1 us
    all_to_all x1, starting transfers between devices, shards(): lax.all_to_all(jnp.stack([a0 for _ in range(lax.axis_size('space'))], axi...  15.5 us
    dot_general x54, matrix products, convolve(): jnp.dot(window.reshape(-1, channels), weights_tap, preferred_element_type...  12.5 us
  transfers between devices with their start and end apart: 16, of which 10 were waited for; matrix products, arithmetic and copies ran while one was open for 2% of the time, Pallas kernels for 0%

profile of v1, /device:TPU:24, one launch (start us, length us, event | category | flops | bytes accessed | tf_op | source)
XLA Modules:
  0.0 579.8 jit_solution(18402464837521828081)
XLA Ops:
  7.3 0.7 all-gather.4.cloned.1.call-update
  8.0 50.1 %all-gather.4.cloned.1.call-done = bf16[16,2,216,256]{3,2,1,0:T(8,128)(2,1)} async-done(((bf16[1,2,216,256]{3,2,1,0:T(8,128)(2,1)}), bf16[16,2,216,256]{3,2,1,0:T(8,128)(2,1)}) %all-gather.4.cloned.1.call-update) | async-done | bytes 3538960 | tf_op jit(solution)/shard_map/all_gather | solution.py:18
  58.1 2.6 convert_reduce_fusion
  60.7 0.4 fusion.43
  61.1 0.7 fusion.129
  61.9 0.7 all-gather.6.cloned.1.call-update
  62.8 0.5 fusion.130
  67.2 36.3 %all-gather.8.cloned.1.call-done = bf16[16,216,256]{2,1,0:T(8,128)(2,1)} async-done(((bf16[1,216,256]{2,1,0:T(8,128)(2,1)}), bf16[16,216,256]{2,1,0:T(8,128)(2,1)}) %all-gather.8.cloned.1.call-update) | async-done | bytes 1769488 | tf_op jit(solution)/shard_map/all_gather | solution.py:23
  103.4 0.9 constant_dynamic-slice_fusion
  104.4 43.1 %all-gather.6.cloned.1.call-done = bf16[16,216,256]{2,1,0:T(8,128)(2,1)} async-done(((bf16[1,216,256]{2,1,0:T(8,128)(2,1)}), bf16[16,216,256]{2,1,0:T(8,128)(2,1)}) %all-gather.6.cloned.1.call-update) | async-done | bytes 1769488 | tf_op jit(solution)/shard_map/all_gather | solution.py:23
  147.5 0.9 constant_dynamic-slice_fusion.1
  148.4 3.4 stack.13
  151.8 15.5 %all-to-all-start = ((bf16[32,2,216,256]{3,2,1,0:T(8,128)(2,1)}), bf16[32,2,216,256]{3,2,1,0:T(8,128)(2,1)}, u32[]{:S(2)}, u32[]{:S(2)}) async-start(bf16[32,2,216,256]{3,2,1,0:T(8,128)(2,1)} %stack.13), calls=%async_computation | async-start | bytes 14155776 | tf_op jit(solution)/shard_map/all_to_all | solution.py:108
  167.3 7.3 %collective-permute-start = (bf16[1,4,16,256]{3,2,1,0:T(8,128)(2,1)S(1)}, bf16[1,4,16,256]{3,2,1,0:T(8,128)(2,1)S(1)}, u32[]{:S(2)}, u32[]{:S(2)}) collective-permute-start(bf16[1,4,16,256]{3,2,1,0:T(8,128)(2,1)S(1)} %get-tuple-element.80), channel_id=1, source_target_pairs={{0,64},{16,80},{32,96},{48,112},{64,128},{80,144},{96,160},{112,17... | collective-permute-start | bytes 98312 | tf_op jit(solution)/shard_map/ppermute | solution.py:14
  174.6 4.9 collective-permute-start.1
  179.5 293.9 %collective-permute-done = bf16[1,4,16,256]{3,2,1,0:T(8,128)(2,1)S(1)} collective-permute-done((bf16[1,4,16,256]{3,2,1,0:T(8,128)(2,1)S(1)}, bf16[1,4,16,256]{3,2,1,0:T(8,128)(2,1)S(1)}, u32[]{:S(2)}, u32[]{:S(2)}) %collective-permute-start) | collective-permute-done | bytes 32800 | tf_op jit(solution)/shard_map/ppermute | solution.py:14
  473.4 8.0 %collective-permute-start.2 = (bf16[10,1,16,256]{3,2,1,0:T(8,128)(2,1)S(1)}, bf16[10,1,16,256]{3,2,1,0:T(8,128)(2,1)S(1)}, u32[]{:S(2)}, u32[]{:S(2)}) collective-permute-start(bf16[10,1,16,256]{3,2,1,0:T(8,128)(2,1)S(1)} %get-tuple-element.72), channel_id=1, source_target_pairs={{0,32},{16,48},{32,64},{48,80},{64,96},{80,112},{96,128},{112,144}... | collective-permute-start | bytes 245768 | tf_op jit(solution)/shard_map/ppermute | solution.py:14
  481.4 2.9 collective-permute-start.3
  484.3 0.8 pad_maximum_fusion.6
  485.2 4.2 collective-permute-done.3
  489.5 8.1 %collective-permute-start.5 = (bf16[10,6,1,256]{3,2,1,0:T(2,128)(2,1)S(1)}, bf16[10,6,1,256]{3,2,1,0:T(2,128)(2,1)S(1)}, u32[]{:S(2)}, u32[]{:S(2)}) collective-permute-start(bf16[10,6,1,256]{3,2,1,0:T(2,128)(2,1)S(1)} %get-tuple-element.50), channel_id=1, source_target_pairs={{16,0},{32,16},{48,32},{64,48},{80,64},{96,80},{112,96},{128,112},... | collective-permute-start | bytes 92168 | tf_op jit(solution)/shard_map/ppermute | solution.py:14
  497.6 1.9 collective-permute-start.4
  499.6 1.1 fusion.126
  500.8 6.6 %collective-permute-done.4 = bf16[10,6,1,256]{3,2,1,0:T(2,128)(2,1)S(1)} collective-permute-done((bf16[10,6,1,256]{3,2,1,0:T(2,128)(2,1)S(1)}, bf16[10,6,1,256]{3,2,1,0:T(2,128)(2,1)S(1)}, u32[]{:S(2)}, u32[]{:S(2)}) %collective-permute-start.4) | collective-permute-done | bytes 30752 | tf_op jit(solution)/shard_map/ppermute | solution.py:14
  507.4 0.4 pad_maximum_fusion
  507.9 2.0 fusion.122
  509.8 1.1 fusion.33
  510.9 0.9 fusion.185
  512.0 0.9 fusion.184
  513.1 3.6 fusion.119
  518.9 0.2 convolution_add_fusion.42
  521.9 0.4 fusion.8
  522.3 0.3 copy-done.20
  524.0 1.9 collective-permute-start.6
  525.9 0.7 fusion.114
  526.6 10.2 %collective-permute-start.7 = (bf16[1,4,16,256]{3,2,1,0:T(8,128)(2,1)S(1)}, bf16[1,4,16,256]{3,2,1,0:T(8,128)(2,1)S(1)}, u32[]{:S(2)}, u32[]{:S(2)}) collective-permute-start(bf16[1,4,16,256]{3,2,1,0:T(8,128)(2,1)S(1)} %get-tuple-element.77), channel_id=1, source_target_pairs={{64,0},{80,16},{96,32},{112,48},{128,64},{144,80},{160,96},{176,11... | collective-permute-start | bytes 98312 | tf_op jit(solution)/shard_map/ppermute | solution.py:14
  536.9 1.5 collective-permute-done.7
  538.4 1.9 collective-permute-start.8
  540.4 8.4 %collective-permute-start.9 = (bf16[10,1,16,256]{3,2,1,0:T(8,128)(2,1)S(1)}, bf16[10,1,16,256]{3,2,1,0:T(8,128)(2,1)S(1)}, u32[]{:S(2)}, u32[]{:S(2)}) collective-permute-start(bf16[10,1,16,256]{3,2,1,0:T(8,128)(2,1)S(1)} %get-tuple-element.69), channel_id=1, source_target_pairs={{32,0},{48,16},{64,32},{80,48},{96,64},{112,80},{128,96},{144,112}... | collective-permute-start | bytes 245768 | tf_op jit(solution)/shard_map/ppermute | solution.py:14
  548.9 0.4 collective-permute-done.8
  549.3 1.7 collective-permute-done.9
  551.2 3.7 collective-permute-start.11
  554.9 2.3 collective-permute-start.10
  557.5 7.3 %collective-permute-done.10 = bf16[10,6,1,256]{3,2,1,0:T(2,128)(2,1)S(1)} collective-permute-done((bf16[10,6,1,256]{3,2,1,0:T(2,128)(2,1)S(1)}, bf16[10,6,1,256]{3,2,1,0:T(2,128)(2,1)S(1)}, u32[]{:S(2)}, u32[]{:S(2)}) %collective-permute-start.10) | collective-permute-done | bytes 30752 | tf_op jit(solution)/shard_map/ppermute | solution.py:14
  564.8 0.4 pad_maximum_fusion.1
  565.3 0.5 fusion.120
  569.1 0.3 convolution_add_fusion.13
  572.4 0.9 fusion.32
  (137 shorter events, 13.7 us)
Async XLA Ops:
  7.2 53.5 %copy-start.1 = (f32[1,2,216,256]{3,2,1,0:T(8,128)S(1)}, f32[1,2,216,256]{3,2,1,0:T(8,128)}, u32[]{:S(2)}) copy-start(f32[1,2,216,256]{3,2,1,0:T(8,128)} %param.10) | copy-start | bytes 1327108
  7.2 53.5 %copy-start.2 = (f32[1,2,216,256]{3,2,1,0:T(8,128)S(1)}, f32[1,2,216,256]{3,2,1,0:T(8,128)}, u32[]{:S(2)}) copy-start(f32[1,2,216,256]{3,2,1,0:T(8,128)} %param.9) | copy-start | bytes 1327108
  7.2 53.5 %copy-start.22 = (f32[2,216,256]{2,1,0:T(8,128)S(1)}, f32[2,216,256]{2,1,0:T(8,128)}, u32[]{:S(2)}) copy-start(f32[2,216,256]{2,1,0:T(8,128)} %param.8) | copy-start | bytes 1327108
  7.2 55.4 %copy-start.23 = (s32[2,32]{1,0:T(2,128)S(1)}, s32[2,32]{1,0:T(2,128)}, u32[]{:S(2)}) copy-start(s32[2,32]{1,0:T(2,128)} %param.11) | copy-start | bytes 772
  7.2 50.9 %all-gather.4.cloned.1.call-start = ((), (), s32[]{:S(2)}) async-start(), calls=%async_computation.1 | async-start | bytes 3760128 | tf_op jit(solution)/shard_map/all_gather | solution.py:18
  7.9 95.5 %all-gather.8.cloned.1.call-start = ((), (), s32[]{:S(2)}) async-start(), calls=%async_computation.3 | async-start | bytes 1880064 | tf_op jit(solution)/shard_map/all_gather | solution.py:23
  61.8 85.6 %all-gather.6.cloned.1.call-start = ((), (), s32[]{:S(2)}) async-start(), calls=%async_computation.2 | async-start | bytes 1880064 | tf_op jit(solution)/shard_map/all_gather | solution.py:23
  151.8 15.5 %copy-start = (bf16[1,1,8,4,16,256]{5,4,3,2,1,0:T(8,128)(2,1)S(1)}, bf16[1,1,8,4,16,256]{5,4,3,2,1,0:T(8,128)(2,1)}, u32[]{:S(2)}) copy-start(bf16[1,1,8,4,16,256]{5,4,3,2,1,0:T(8,128)(2,1)} %param.6) | copy-start | bytes 786436
  151.8 361.3 %all-to-all-start = ((bf16[32,2,216,256]{3,2,1,0:T(8,128)(2,1)}), bf16[32,2,216,256]{3,2,1,0:T(8,128)(2,1)}, u32[]{:S(2)}, u32[]{:S(2)}) async-start(bf16[32,2,216,256]{3,2,1,0:T(8,128)(2,1)} %stack.13), calls=%async_computation | async-start | bytes 14155776 | tf_op jit(solution)/shard_map/all_to_all | solution.py:108
  167.3 306.1 %collective-permute-start = (bf16[1,4,16,256]{3,2,1,0:T(8,128)(2,1)S(1)}, bf16[1,4,16,256]{3,2,1,0:T(8,128)(2,1)S(1)}, u32[]{:S(2)}, u32[]{:S(2)}) collective-permute-start(bf16[1,4,16,256]{3,2,1,0:T(8,128)(2,1)S(1)} %get-tuple-element.80), channel_id=1, source_target_pairs={{0,64},{16,80},{32,96},{48,112},{64,128},{80,144},{96,160},{112,17... | collective-permute-start | bytes 98312 | tf_op jit(solution)/shard_map/ppermute | solution.py:14
  174.6 298.8 %collective-permute-start.1 = (bf16[1,4,16,256]{3,2,1,0:T(8,128)(2,1)S(1)}, bf16[1,4,16,256]{3,2,1,0:T(8,128)(2,1)S(1)}, u32[]{:S(2)}, u32[]{:S(2)}) collective-permute-start(bf16[1,4,16,256]{3,2,1,0:T(8,128)(2,1)S(1)} %get-tuple-element.81), channel_id=1, source_target_pairs={{64,0},{80,16},{96,32},{112,48},{128,64},{144,80},{160,96},{176,11... | collective-permute-start | bytes 98312 | tf_op jit(solution)/shard_map/ppermute | solution.py:14
  473.4 11.7 %collective-permute-start.2 = (bf16[10,1,16,256]{3,2,1,0:T(8,128)(2,1)S(1)}, bf16[10,1,16,256]{3,2,1,0:T(8,128)(2,1)S(1)}, u32[]{:S(2)}, u32[]{:S(2)}) collective-permute-start(bf16[10,1,16,256]{3,2,1,0:T(8,128)(2,1)S(1)} %get-tuple-element.72), channel_id=1, source_target_pairs={{0,32},{16,48},{32,64},{48,80},{64,96},{80,112},{96,128},{112,144}... | collective-permute-start | bytes 245768 | tf_op jit(solution)/shard_map/ppermute | solution.py:14
  481.4 7.9 %collective-permute-start.3 = (bf16[10,1,16,256]{3,2,1,0:T(8,128)(2,1)S(1)}, bf16[10,1,16,256]{3,2,1,0:T(8,128)(2,1)S(1)}, u32[]{:S(2)}, u32[]{:S(2)}) collective-permute-start(bf16[10,1,16,256]{3,2,1,0:T(8,128)(2,1)S(1)} %get-tuple-element.73), channel_id=1, source_target_pairs={{32,0},{48,16},{64,32},{80,48},{96,64},{112,80},{128,96},{144,112}... | collective-permute-start | bytes 245768 | tf_op jit(solution)/shard_map/ppermute | solution.py:14
  489.5 11.2 %collective-permute-start.5 = (bf16[10,6,1,256]{3,2,1,0:T(2,128)(2,1)S(1)}, bf16[10,6,1,256]{3,2,1,0:T(2,128)(2,1)S(1)}, u32[]{:S(2)}, u32[]{:S(2)}) collective-permute-start(bf16[10,6,1,256]{3,2,1,0:T(2,128)(2,1)S(1)} %get-tuple-element.50), channel_id=1, source_target_pairs={{16,0},{32,16},{48,32},{64,48},{80,64},{96,80},{112,96},{128,112},... | collective-permute-start | bytes 92168 | tf_op jit(solution)/shard_map/ppermute | solution.py:14
  497.6 9.7 %collective-permute-start.4 = (bf16[10,6,1,256]{3,2,1,0:T(2,128)(2,1)S(1)}, bf16[10,6,1,256]{3,2,1,0:T(2,128)(2,1)S(1)}, u32[]{:S(2)}, u32[]{:S(2)}) collective-permute-start(bf16[10,6,1,256]{3,2,1,0:T(2,128)(2,1)S(1)} %get-tuple-element.51), channel_id=1, source_target_pairs={{0,16},{16,32},{32,48},{48,64},{64,80},{80,96},{96,112},{112,128},... | collective-permute-start | bytes 92168 | tf_op jit(solution)/shard_map/ppermute | solution.py:14
  513.1 3.6 copy-start.4
  513.1 3.8 copy-start.3
  517.0 1.9 copy-start.11
  517.4 1.7 copy-start.19
  517.7 1.7 copy-start.18
  518.2 1.5 copy-start.21
  518.6 1.3 copy-start.17
  518.9 1.3 copy-start.16
  519.1 1.3 copy-start.7
  519.4 1.3 copy-start.15
  519.6 1.2 copy-start.14
  519.9 1.2 copy-start.6
  520.1 1.2 copy-start.13
  520.4 1.2 copy-start.12
  521.6 1.0 copy-start.20
  521.9 1.0 copy-start.10
  521.9 1.2 copy-start.9
  522.3 1.0 copy-start.5
  522.3 1.3 copy-start.8
  524.0 12.9 %collective-permute-start.6 = (bf16[1,4,16,256]{3,2,1,0:T(8,128)(2,1)S(1)}, bf16[1,4,16,256]{3,2,1,0:T(8,128)(2,1)S(1)}, u32[]{:S(2)}, u32[]{:S(2)}) collective-permute-start(bf16[1,4,16,256]{3,2,1,0:T(8,128)(2,1)S(1)} %get-tuple-element.76), channel_id=1, source_target_pairs={{0,64},{16,80},{32,96},{48,112},{64,128},{80,144},{96,160},{112,17... | collective-permute-start | bytes 98312 | tf_op jit(solution)/shard_map/ppermute | solution.py:14
  526.6 11.8 %collective-permute-start.7 = (bf16[1,4,16,256]{3,2,1,0:T(8,128)(2,1)S(1)}, bf16[1,4,16,256]{3,2,1,0:T(8,128)(2,1)S(1)}, u32[]{:S(2)}, u32[]{:S(2)}) collective-permute-start(bf16[1,4,16,256]{3,2,1,0:T(8,128)(2,1)S(1)} %get-tuple-element.77), channel_id=1, source_target_pairs={{64,0},{80,16},{96,32},{112,48},{128,64},{144,80},{160,96},{176,11... | collective-permute-start | bytes 98312 | tf_op jit(solution)/shard_map/ppermute | solution.py:14
  538.4 10.8 %collective-permute-start.8 = (bf16[10,1,16,256]{3,2,1,0:T(8,128)(2,1)S(1)}, bf16[10,1,16,256]{3,2,1,0:T(8,128)(2,1)S(1)}, u32[]{:S(2)}, u32[]{:S(2)}) collective-permute-start(bf16[10,1,16,256]{3,2,1,0:T(8,128)(2,1)S(1)} %get-tuple-element.68), channel_id=1, source_target_pairs={{0,32},{16,48},{32,64},{48,80},{64,96},{80,112},{96,128},{112,144}... | collective-permute-start | bytes 245768 | tf_op jit(solution)/shard_map/ppermute | solution.py:14
  540.4 10.6 %collective-permute-start.9 = (bf16[10,1,16,256]{3,2,1,0:T(8,128)(2,1)S(1)}, bf16[10,1,16,256]{3,2,1,0:T(8,128)(2,1)S(1)}, u32[]{:S(2)}, u32[]{:S(2)}) collective-permute-start(bf16[10,1,16,256]{3,2,1,0:T(8,128)(2,1)S(1)} %get-tuple-element.69), channel_id=1, source_target_pairs={{32,0},{48,16},{64,32},{80,48},{96,64},{112,80},{128,96},{144,112}... | collective-permute-start | bytes 245768 | tf_op jit(solution)/shard_map/ppermute | solution.py:14
  551.2 6.2 %collective-permute-start.11 = (bf16[10,6,1,256]{3,2,1,0:T(2,128)(2,1)S(1)}, bf16[10,6,1,256]{3,2,1,0:T(2,128)(2,1)S(1)}, u32[]{:S(2)}, u32[]{:S(2)}) collective-permute-start(bf16[10,6,1,256]{3,2,1,0:T(2,128)(2,1)S(1)} %get-tuple-element.46), channel_id=1, source_target_pairs={{16,0},{32,16},{48,32},{64,48},{80,64},{96,80},{112,96},{128,112},... | collective-permute-start | bytes 92168 | tf_op jit(solution)/shard_map/ppermute | solution.py:14
  554.9 9.8 %collective-permute-start.10 = (bf16[10,6,1,256]{3,2,1,0:T(2,128)(2,1)S(1)}, bf16[10,6,1,256]{3,2,1,0:T(2,128)(2,1)S(1)}, u32[]{:S(2)}, u32[]{:S(2)}) collective-permute-start(bf16[10,6,1,256]{3,2,1,0:T(2,128)(2,1)S(1)} %get-tuple-element.47), channel_id=1, source_target_pairs={{0,16},{16,32},{32,48},{48,64},{64,80},{80,96},{96,112},{112,128},... | collective-permute-start | bytes 92168 | tf_op jit(solution)/shard_map/ppermute | solution.py:14
Sparse Core Ops, SparseCore 0:
  10.2 47.9 all-gather.3
  61.9 41.4 all-gather.7
  106.2 41.2 all-gather.5
